TPU v7x, 32 devices: a whole 2x2x4 slice. The times are simulated.
32 devices in a mesh: ctx: 16 (over z, y, core), head: 2 (over x).
Axes of the slice: x: 2, y: 2, z: 4, core: 2. Of those that a mesh axis runs over, the one named last changes fastest.
Arguments:
- events: bfloat16 [4096, 1024], P('ctx'), may hold values from -8 to 8
- ssm_input: bfloat16 [4096, 2048], P('ctx', 'head'), may hold values from -1.5 to 1.5
- gate_input: bfloat16 [4096, 2048], P('ctx', 'head'), may hold values from -6 to 6
- grad_out: bfloat16 [4096, 2048], P('ctx', 'head'), may hold values from -0.015625 to 0.015625
- shared_b: bfloat16 [4096, 128], P('ctx'), may hold values from -6 to 6
- shared_c: bfloat16 [4096, 128], P('ctx'), may hold values from -6 to 6
- log_decay: float32 [32, 4096], P('head', 'ctx'), may hold values from -1 to 0, as said below
- entry_state: float32 [16, 32, 128, 64], P('ctx', 'head'), may hold values from -48 to 48
- w_gate: bfloat16 [1024, 2048], P(None, 'head'), may hold values from -0.1875 to 0.1875
- w_value: bfloat16 [1024, 2048], P(None, 'head'), may hold values from -0.1875 to 0.1875
- w_shared: bfloat16 [1024, 256], P(None, 'head'), may hold values from -0.1875 to 0.1875
Outputs:
- grad_input: bfloat16 [4096, 1024], P('ctx', 'head')
- grad_w_gate: float32 [1024, 2048], P('ctx', 'head')
- grad_w_value: float32 [1024, 2048], P('ctx', 'head')
- grad_w_shared: float32 [1024, 256], P('ctx', 'head')
Inputs may be any that keep to these rules, and one draw needn't show every extreme that they name: `log_decay`: every entry is negative.
All inputs are finite; a program needn't handle non-finite values.
Results may differ from a plain program's by a relative error of at most 0.015.
Values may be sent and summed in bfloat16 or wider, within the bound.
A program may use at most 64 MiB of HBM per device.

v0:
```python
import math

import jax
import jax.numpy as jnp
from jax import lax
from jax.sharding import PartitionSpec as P

SPAN = 256


highest = lax.Precision.HIGHEST


def entering(part, axis, combine, identity):
    count = lax.axis_size(axis)
    place = lax.axis_index(axis)
    ahead = count - 1 - place
    gathered = jax.tree.map(lambda a: lax.all_gather(a, axis), part)
    state = jax.tree.map(lambda a, e: jnp.zeros_like(a) + jnp.asarray(e, a.dtype), part, identity)

    def one(lap, state):
        source = count - 1 - lap
        return combine(
            state, jax.tree.map(lambda a: lax.dynamic_index_in_dim(a, source, 0, False), gathered)
        )

    return lax.fori_loop(0, ahead, one, state)


def ssd_partials(ssm_input, gate_input, grad_out, shared_b, shared_c, log_decay, entry, block_len):
    head_count, length = log_decay.shape
    head_width = ssm_input.shape[1] // head_count
    span_count = length // block_len
    values_f = ssm_input.astype(jnp.float32).reshape(span_count, block_len, head_count, head_width)
    gates_f = gate_input.astype(jnp.float32).reshape(span_count, block_len, head_count, head_width)
    grad_f = grad_out.astype(jnp.float32).reshape(span_count, block_len, head_count, head_width)
    shared_bf = shared_b.astype(jnp.float32).reshape(span_count, block_len, shared_b.shape[1])
    shared_cf = shared_c.astype(jnp.float32).reshape(span_count, block_len, shared_c.shape[1])
    cumlog = jnp.cumsum(log_decay.reshape(head_count, span_count, block_len), axis=2)
    totals = cumlog[:, :, -1]
    causal = jnp.arange(block_len)[:, None] >= jnp.arange(block_len)[None, :]
    spread = cumlog[:, :, :, None] - cumlog[:, :, None, :]
    decay_mat = jnp.where(causal, jnp.exp(jnp.minimum(spread, 0.0)), 0.0)
    shared_c_blocks = shared_c.reshape(span_count, block_len, shared_c.shape[1])
    shared_b_blocks = shared_b.reshape(span_count, block_len, shared_b.shape[1])
    scores = jnp.einsum(
        "ktn,ksn->kts", shared_c_blocks, shared_b_blocks, preferred_element_type=jnp.float32
    )
    weighted = decay_mat * scores[None]
    to_end = jnp.exp(totals[:, :, None] - cumlog).transpose(1, 2, 0)
    from_start = jnp.exp(cumlog).transpose(1, 2, 0)
    scaled_x = values_f * to_end[..., None]
    local_states = jnp.einsum("ksn,kshp->khnp", shared_bf, scaled_x, precision=highest)
    span_decay = jnp.exp(totals).T

    def forward_step(running, inputs):
        decay_k, local_k = inputs
        return (decay_k[:, None, None] * running + local_k, running)

    _, entries = lax.scan(forward_step, entry, (span_decay, local_states))
    ssm_out = jnp.einsum("hkts,kshp->kthp", weighted, values_f, precision=highest)
    ssm_out = ssm_out + from_start[..., None] * jnp.einsum(
        "ktn,khnp->kthp", shared_cf, entries, precision=highest
    )
    gate_sig = jax.nn.sigmoid(gates_f)
    grad_y = grad_f * gates_f * gate_sig
    grad_z = grad_f * ssm_out * gate_sig * (1.0 + gates_f * (1.0 - gate_sig))
    products = decay_mat * jnp.einsum("kthp,kshp->hkts", grad_y, values_f, precision=highest)
    scaled_dy = grad_y * from_start[..., None]
    grad_c = jnp.einsum("hkts,ksn->ktn", products, shared_bf, precision=highest)
    grad_c = grad_c + jnp.einsum("kthp,khnp->ktn", scaled_dy, entries, precision=highest)
    grad_b = jnp.einsum("hkst,ksn->ktn", products, shared_cf, precision=highest)
    grad_x = jnp.einsum("hkst,kshp->kthp", weighted, grad_y, precision=highest)
    block_terms = jnp.einsum("ksn,kshp->khnp", shared_cf, scaled_dy, precision=highest)

    def backward_step(running, inputs):
        decay_k, term_k = inputs
        return (term_k + decay_k[:, None, None] * running, running)

    block_sum, later_sums = lax.scan(
        backward_step, jnp.zeros_like(entry), (span_decay, block_terms), reverse=True
    )
    block_log = jnp.sum(totals, axis=1)
    suffix = block_log[None, :] - jnp.cumsum(totals, axis=1).T
    grad_z_out = grad_z.reshape(length, head_count * head_width).astype(jnp.bfloat16)
    return (
        grad_z_out,
        grad_x,
        grad_b,
        grad_c,
        later_sums,
        suffix,
        to_end,
        scaled_x,
        shared_bf,
        block_sum,
        block_log,
    )


def finish_block(partials, incoming):
    (
        grad_z_out,
        grad_x,
        grad_b,
        grad_c,
        later_sums,
        suffix,
        to_end,
        scaled_x,
        shared_bf,
        block_sum,
        block_log,
    ) = partials
    carried = later_sums + jnp.exp(suffix)[:, :, None, None] * incoming[None]
    grad_x = grad_x + to_end[..., None] * jnp.einsum(
        "ktn,khnp->kthp", shared_bf, carried, precision=highest
    )
    grad_b = grad_b + jnp.einsum("kthp,khnp->ktn", scaled_x, carried, precision=highest)
    length = grad_z_out.shape[0]
    grad_x_out = grad_x.reshape(length, grad_z_out.shape[1]).astype(jnp.bfloat16)
    grad_bc = jnp.concatenate([grad_b.reshape(length, -1), grad_c.reshape(length, -1)], axis=1)
    return (grad_z_out, grad_x_out, grad_bc)


def times_rows(left, weights):
    return lax.dot_general(
        left, weights, (((1,), (1,)), ((), ())), preferred_element_type=jnp.float32
    )


def row_term(events, projected, norm_scale):
    return (
        lax.dot_general(
            events, projected, (((0,), (0,)), ((), ())), preferred_element_type=jnp.float32
        )
        * norm_scale
    )


def per_device(
    events,
    ssm_input,
    gate_input,
    grad_out,
    shared_b,
    shared_c,
    log_decay,
    entry_state,
    w_gate,
    w_value,
    w_shared,
):
    partials = ssd_partials(
        ssm_input, gate_input, grad_out, shared_b, shared_c, log_decay, entry_state[0], SPAN
    )
    grad_z = partials[0]
    block_sum = partials[9]
    block_log = partials[10]

    def combine(earlier_part, later_part):
        return (
            earlier_part[0] * later_part[0],
            later_part[1] + later_part[0][:, None, None] * earlier_part[1],
        )

    identity = (jnp.ones_like(block_log), jnp.zeros_like(block_sum))
    _, incoming = entering((jnp.exp(block_log), block_sum), "ctx", combine, identity)
    grad_z, grad_x, grad_bc_part = finish_block(partials, incoming)
    grad_bc = lax.psum_scatter(grad_bc_part, "head", scatter_dimension=1, tiled=True).astype(
        jnp.bfloat16
    )
    input_part = (
        times_rows(grad_z, w_gate) + times_rows(grad_x, w_value) + times_rows(grad_bc, w_shared)
    )
    grad_input = lax.psum_scatter(
        input_part.astype(jnp.bfloat16), "head", scatter_dimension=1, tiled=True
    )
    norm_scale = 1.0 / math.sqrt(events.shape[0] * lax.axis_size("ctx"))
    head_cols = grad_z.shape[1]
    projected = jnp.concatenate([grad_z, grad_x, grad_bc], axis=1)
    reduced = lax.psum_scatter(
        row_term(events, projected, norm_scale), "ctx", scatter_dimension=0, tiled=True
    )
    grad_w_gate = reduced[:, :head_cols]
    grad_w_value = reduced[:, head_cols : 2 * head_cols]
    grad_w_shared = reduced[:, 2 * head_cols :]
    return (grad_input, grad_w_gate, grad_w_value, grad_w_shared)


def solution(mesh):
    placed = (
        P("ctx", None),
        P("ctx", "head"),
        P("ctx", "head"),
        P("ctx", "head"),
        P("ctx", None),
        P("ctx", None),
        P("head", "ctx"),
        P("ctx", "head", None, None),
        P(None, "head"),
        P(None, "head"),
        P(None, "head"),
    )
    return jax.shard_map(
        per_device,
        mesh=mesh,
        in_specs=placed,
        out_specs=(P("ctx", "head"), P("ctx", "head"), P("ctx", "head"), P("ctx", "head")),
        check_vma=False,
    )
```

profile of v0, /device:TPU:0, one launch (start us, length us, event | category | flops | bytes accessed | tf_op | source)
XLA Modules:
  0.0 362.0 jit_solution(16537649130431571565)
XLA Ops:
  9.5 2.1 copy.70
  11.6 2.1 copy.64
  13.7 2.6 divide_multiply_fusion
  16.3 1.4 fusion.46
  19.4 35.5 %all-reduce = f32[256]{0:T(256)S(1)} all-reduce(f32[256]{0:T(256)S(1)} %dynamic-update-slice), channel_id=2, replica_groups=mesh['ctx'=16,'head'=2] {'ctx'}, use_global_device_ids=true, to_apply=%add | all-reduce | flops 256 | bytes 2048
  55.6 2.0 copy.68
  57.6 2.1 bitcast_multiply_fusion
  59.7 2.1 convolution_bitcast_fusion.2
  63.3 4.4 %multiply_reduce_fusion = f32[256,256]{1,0:T(8,128)S(1)} fusion(f32[256,16,64]{0,2,1:T(8,128)} %bitcast.143, bf16[256,16,64]{0,2,1:T(8,128)(2,1)} %bitcast.139, f32[16,256]{1,0:T(8,128)S(1)} %bitcast_add_fusion.1, pred[256,256]{1,0:T(8,128)(4,1)S(1)} %iota_compare_fusion), kind=kOutput, calls=%fused_computation.4 | convolution fusion | flops 810483712 | bytes 1916928 | tf_op jit(solution)/shard_map/kthp,kshp->hkts/dot_general | solution.py:68
  68.7 1.6 fusion.65
  70.2 25.4 %all-gather.3.cloned.1.call-done = f32[16,16,128,64]{2,3,1,0:T(8,128)} async-done(((f32[1,16,128,64]{2,3,1,0:T(8,128)}), f32[16,16,128,64]{2,3,1,0:T(8,128)}) %all-gather.3.cloned.1.call-update) | async-done | bytes 8388624 | tf_op jit(solution)/shard_map/all_gather | solution.py:18
  96.8 103.8 %while.9 = (s32[]{:T(128)}, f32[16,128,64]{2,1,0:T(8,128)}, s32[]{:T(128)}, f32[16,16,128,64]{2,3,1,0:T(8,128)}, f32[16,16]{1,0:T(8,128)}, /*index=5*/s32[]{:T(128)}, s32[]{:T(128)}, s32[]{:T(128)}, s32[]{:T(128)}) while((s32[]{:T(128)}, f32[16,128,64]{2,1,0:T(8,128)}, s32[]{:T(128)}, f32[16,16,128,64]{2,3,1,0:T(8,128)}, f32[16,16]{1,0:T(8,128)}, ...), condition=%wide.region_3.4_spmd, body=%wide.region_2.3_spmd.sunk | while | flops 262150 | bytes 3670363 | solution.py:27
  98.0 1.9 constant_dynamic-slice_fusion.2
  99.9 1.4 copy.97
  101.3 2.4 bitcast_add_fusion.3
  105.0 1.9 constant_dynamic-slice_fusion.2
  106.8 1.4 copy.97
  108.2 2.4 bitcast_add_fusion.3
  111.9 1.9 constant_dynamic-slice_fusion.2
  113.8 1.4 copy.97
  115.2 2.4 bitcast_add_fusion.3
  118.8 1.9 constant_dynamic-slice_fusion.2
  120.7 1.4 copy.97
  122.1 2.4 bitcast_add_fusion.3
  125.7 1.9 constant_dynamic-slice_fusion.2
  127.6 1.4 copy.97
  129.0 2.4 bitcast_add_fusion.3
  132.7 1.9 constant_dynamic-slice_fusion.2
  134.5 1.4 copy.97
  135.9 2.4 bitcast_add_fusion.3
  139.6 1.9 constant_dynamic-slice_fusion.2
  141.5 1.4 copy.97
  142.8 2.4 bitcast_add_fusion.3
  146.5 1.9 constant_dynamic-slice_fusion.2
  148.4 1.4 copy.97
  149.8 2.4 bitcast_add_fusion.3
  153.4 1.9 constant_dynamic-slice_fusion.2
  156.7 2.4 bitcast_add_fusion.3
  160.3 1.9 constant_dynamic-slice_fusion.2
  162.2 1.4 copy.97
  163.6 2.4 bitcast_add_fusion.3
  167.3 1.9 constant_dynamic-slice_fusion.2
  169.1 1.4 copy.97
  170.5 2.4 bitcast_add_fusion.3
  174.2 1.9 constant_dynamic-slice_fusion.2
  176.1 1.4 copy.97
  177.4 2.4 bitcast_add_fusion.3
  181.1 1.9 constant_dynamic-slice_fusion.2
  184.4 2.4 bitcast_add_fusion.3
  188.0 1.9 constant_dynamic-slice_fusion.2
  189.9 1.4 copy.97
  191.3 2.4 bitcast_add_fusion.3
  194.9 1.9 constant_dynamic-slice_fusion.2
  196.8 1.4 copy.97
  198.2 2.4 bitcast_add_fusion.3
  200.6 2.9 convolution_bitcast_fusion.3
  203.8 1.6 pad_maximum_fusion
  205.7 5.8 %fusion.42 = bf16[1,256,16,64]{1,3,2,0:T(8,128)(2,1)S(1)} fusion(bf16[256,16,64]{0,2,1:T(8,128)(2,1)} %bitcast.140, f32[256,256]{1,0:T(8,128)} %fusion.64, f32[16,256]{1,0:T(8,128)} %copy-done.12, pred[256,256]{1,0:T(8,128)(4,1)} %copy-done.10, f32[256,16,64]{0,2,1:T(8,128)} %bitcast.145, f32[256,16]{0,1:T(8,128)} %bitcast.151, ...), kind=kOutput, calls=%fused_computation.33 | convolution fusion | flops 813170688 | bytes 3506176 | tf_op jit(solution)/shard_map/hkts,kshp->kthp/dot_general | solution.py:61
  212.7 3.9 %fusion.38 = bf16[1,256,16,64]{1,3,2,0:T(8,128)(2,1)S(1)} fusion(f32[1,256,16,64]{1,3,2,0:T(8,128)S(1)} %fusion.22, f32[256,16,64]{0,2,1:T(8,128)S(1)} %bitcast.144, f32[256,256]{1,0:T(8,128)S(1)} %copy-done.7, f32[16,256]{1,0:T(8,128)S(1)} %copy-done.13, pred[256,256]{1,0:T(8,128)(4,1)S(1)} %copy-done.11), kind=kOutput, calls=%fused_computation.31 | convolution fusion | flops 810024960 | bytes 2965504 | tf_op jit(solution)/shard_map/hkst,kshp->kthp/dot_general | solution.py:73
  217.6 5.8 %multiply_bitcast_fusion = f32[1024,2176]{0,1:T(8,128)} fusion(bf16[256,1024]{1,0:T(8,128)(2,1)} %param.13, bf16[256,128]{0,1:T(8,128)(2,1)S(1)} %convert_element_type.36, bf16[256,1024]{0,1:T(8,128)(2,1)S(1)} %bitcast.136, bf16[256,1024]{0,1:T(8,128)(2,1)S(1)} %bitcast.134), kind=kOutput, calls=%fused_computation.3 | convolution fusion | flops 1146421248 | bytes 10551296 | tf_op jit(solution)/shard_map/dot_general | solution.py:134
  223.4 9.3 %copy.80 = f32[1024,2176]{1,0:T(8,128)} copy(f32[1024,2176]{0,1:T(8,128)} %multiply_bitcast_fusion) | data formatting | bytes 17825792
  236.3 102.2 %reduce-scatter.10.cloned.1.call-done = f32[64,2176]{1,0:T(8,128)} async-done(((f32[1024,2176]{1,0:T(8,128)}), f32[64,2176]{1,0:T(8,128)}) %reduce-scatter.10.cloned.1.call-update) | async-done | bytes 557072
  339.8 1.9 fusion.63
  341.7 13.8 %reduce-scatter.8.cloned.1.call-done = bf16[256,512]{1,0:T(8,128)(2,1)} async-done(((bf16[256,1024]{1,0:T(8,128)(2,1)}), bf16[256,512]{1,0:T(8,128)(2,1)}) %reduce-scatter.8.cloned.1.call-update) | async-done | bytes 262160 | tf_op jit(solution)/shard_map/reduce_scatter | solution.py:176
  (90 shorter events, 37.0 us)
Async XLA Ops:
  7.2 225.6 %copy-start = (bf16[1024,1024]{1,0:T(8,128)(2,1)S(1)}, bf16[1024,1024]{1,0:T(8,128)(2,1)}, u32[]{:S(2)}) copy-start(bf16[1024,1024]{1,0:T(8,128)(2,1)} %param.21) | copy-start | bytes 6291460
  7.2 10.7 %copy-start.15 = (u32[32]{0:T(128)S(1)}, u32[32]{0:T(128)}, u32[]{:S(2)}) copy-start(u32[32]{0:T(128)} %constant.79) | copy-start | bytes 388
  7.2 9.1 %copy-start.5 = (bf16[256,128]{1,0:T(8,128)(2,1)S(1)}, bf16[256,128]{1,0:T(8,128)(2,1)}, u32[]{:S(2)}) copy-start(bf16[256,128]{1,0:T(8,128)(2,1)} %param.18) | copy-start | bytes 196612
  7.2 88.5 %all-gather.3.cloned.1.call-start = ((), (), s32[]{:S(2)}) async-start(), calls=%async_computation.3 | async-start | bytes 8912896 | tf_op jit(solution)/shard_map/all_gather | solution.py:18
  9.2 48.4 %copy-start.9 = (f32[1,256,16]{1,2,0:T(8,128)}, f32[1,256,16]{1,2,0:T(8,128)S(1)}, u32[]{:S(2)}) copy-start(f32[1,256,16]{1,2,0:T(8,128)S(1)} %copy.95) | copy-start | bytes 49156
  13.7 48.8 %copy-start.6 = (bf16[256,128]{1,0:T(8,128)(2,1)S(1)}, bf16[256,128]{1,0:T(8,128)(2,1)}, u32[]{:S(2)}) copy-start(bf16[256,128]{1,0:T(8,128)(2,1)} %param.17) | copy-start | bytes 196612
  17.7 198.9 %reduce-scatter.6.cloned.1.call-start = ((), (), s32[]{:S(2)}) async-start(), calls=%async_computation.4 | async-start | bytes 393216 | tf_op jit(solution)/shard_map/reduce_scatter | solution.py:170
  59.7 8.0 %copy-start.10 = (pred[256,256]{1,0:T(8,128)(4,1)}, pred[256,256]{1,0:T(8,128)(4,1)S(1)}, u32[]{:S(2)}) copy-start(pred[256,256]{1,0:T(8,128)(4,1)S(1)} %iota_compare_fusion) | copy-start | bytes 196612
  62.4 6.3 %copy-start.12 = (f32[16,256]{1,0:T(8,128)}, f32[16,256]{1,0:T(8,128)S(1)}, u32[]{:S(2)}) copy-start(f32[16,256]{1,0:T(8,128)S(1)} %bitcast_add_fusion.1) | copy-start | bytes 49156
  63.3 5.4 %copy-start.2 = (f32[1,16,128,64]{2,3,1,0:T(8,128)S(1)}, f32[1,16,128,64]{2,3,1,0:T(8,128)}, u32[]{:S(2)}) copy-start(f32[1,16,128,64]{2,3,1,0:T(8,128)} %param.20) | copy-start | bytes 1572868
  205.4 133.0 %reduce-scatter.10.cloned.1.call-start = ((), (), s32[]{:S(2)}) async-start(), calls=%async_computation.6 | async-start | bytes 9469952
  205.7 5.9 %copy-start.1 = (f32[16,128,64]{2,1,0:T(8,128)S(1)}, f32[16,128,64]{2,1,0:T(8,128)}, u32[]{:S(2)}) copy-start(f32[16,128,64]{2,1,0:T(8,128)} %get-tuple-element.118) | copy-start | bytes 1572868
  205.7 5.9 %copy-start.14 = (f32[16]{0:T(128)S(1)}, f32[16]{0:T(128)}, u32[]{:S(2)}) copy-start(f32[16]{0:T(128)} %subtract_exponential_fusion) | copy-start | bytes 196
  205.7 7.0 %copy-start.4 = (f32[256,1024]{0,1:T(8,128)S(1)}, f32[256,1024]{0,1:T(8,128)}, u32[]{:S(2)}) copy-start(f32[256,1024]{0,1:T(8,128)} %get-tuple-element.170) | copy-start | bytes 3145732
  205.7 7.0 %copy-start.7 = (f32[256,256]{1,0:T(8,128)S(1)}, f32[256,256]{1,0:T(8,128)}, u32[]{:S(2)}) copy-start(f32[256,256]{1,0:T(8,128)} %fusion.64) | copy-start | bytes 786436
  205.7 7.0 %copy-start.11 = (pred[256,256]{1,0:T(8,128)(4,1)S(1)}, pred[256,256]{1,0:T(8,128)(4,1)}, u32[]{:S(2)}) copy-start(pred[256,256]{1,0:T(8,128)(4,1)} %copy-done.10) | copy-start | bytes 196612
  205.7 7.0 %copy-start.13 = (f32[16,256]{1,0:T(8,128)S(1)}, f32[16,256]{1,0:T(8,128)}, u32[]{:S(2)}) copy-start(f32[16,256]{1,0:T(8,128)} %copy-done.12) | copy-start | bytes 49156
  232.7 2.5 copy-start.8
  232.7 122.8 %reduce-scatter.8.cloned.1.call-start = ((), (), s32[]{:S(2)}) async-start(), calls=%async_computation.5 | async-start | bytes 786432 | tf_op jit(solution)/shard_map/reduce_scatter | solution.py:176
  232.7 1.6 copy-start.3
Sparse Core Ops, SparseCore 0:
  17.8 77.8 all-gather.2
  205.6 8.8 reduce-scatter.5
  232.8 105.6 reduce-scatter.9
  341.1 14.2 reduce-scatter.7
where the time goes:
time: 365 us; the launch traced here: 362 us
  waiting for transfers between devices  141 us (39%)
  local copies, waits for them, and re-layouts  91.5 us (25%)
  other arithmetic  44.5 us (12%)
  blocking collectives  35.5 us (10%)
  matrix products  33.7 us (9%)
  between operations  14.8 us (4%)
    unnamed x5, waiting for transfers between devices  102 us
    dynamic_slice x30, local copies, waits for them, and re-layouts, one(): lax.dynamic_index_in_dim(a, source, 0, False)  48.9 us
    add x15, other arithmetic, combine(): later_part[1] + later_part[0][:, None, None] * earlier_part[1]  35.6 us
    unnamed x1, blocking collectives  35.5 us
    all_gather x1, waiting for transfers between devices, entering(): gathered = jax.tree.map(lambda a: lax.all_gather(a, axis), part)  25.4 us
    mul x15, local copies, waits for them, and re-layouts, combine(): later_part[0][:, None, None] * earlier_part[1]  19.2 us
    unnamed x41, local copies, waits for them, and re-layouts  17.2 us
    reduce_scatter x1, waiting for transfers between devices, per_device(): lax.psum_scatter(input_part.astype(jnp.bfloat16), 'head', scatter_dimensi...  13.8 us
  transfers between devices with their start and end apart: 4, of which 3 were waited for; matrix products, arithmetic and copies ran while one was open for 9% of the time, Pallas kernels for 0%

commit v1 on v0

--- a/solution.py
+++ b/solution.py
@@ -11,20 +11,16 @@
 highest = lax.Precision.HIGHEST
 
 
-def entering(part, axis, combine, identity):
+def entering(block_log, block_sum, axis):
     count = lax.axis_size(axis)
     place = lax.axis_index(axis)
-    ahead = count - 1 - place
-    gathered = jax.tree.map(lambda a: lax.all_gather(a, axis), part)
-    state = jax.tree.map(lambda a, e: jnp.zeros_like(a) + jnp.asarray(e, a.dtype), part, identity)
-
-    def one(lap, state):
-        source = count - 1 - lap
-        return combine(
-            state, jax.tree.map(lambda a: lax.dynamic_index_in_dim(a, source, 0, False), gathered)
-        )
-
-    return lax.fori_loop(0, ahead, one, state)
+    logs = lax.all_gather(block_log, axis)
+    sums = lax.all_gather(block_sum.astype(jnp.bfloat16), axis)
+    index = jnp.arange(count)[:, None]
+    between = ((index > index.T) & (index.T > place))[:, :, None]
+    exponent = jnp.sum(jnp.where(between, logs[None], 0.0), axis=1)
+    weight = jnp.where(index > place, jnp.exp(exponent), 0.0)
+    return jnp.sum(weight[:, :, None, None] * sums.astype(jnp.float32), axis=0)
 
 
 def ssd_partials(ssm_input, gate_input, grad_out, shared_b, shared_c, log_decay, entry, block_len):
@@ -158,14 +154,7 @@
     block_sum = partials[9]
     block_log = partials[10]
 
-    def combine(earlier_part, later_part):
-        return (
-            earlier_part[0] * later_part[0],
-            later_part[1] + later_part[0][:, None, None] * earlier_part[1],
-        )
-
-    identity = (jnp.ones_like(block_log), jnp.zeros_like(block_sum))
-    _, incoming = entering((jnp.exp(block_log), block_sum), "ctx", combine, identity)
+    incoming = entering(block_log, block_sum, "ctx")
     grad_z, grad_x, grad_bc_part = finish_block(partials, incoming)
     grad_bc = lax.psum_scatter(grad_bc_part, "head", scatter_dimension=1, tiled=True).astype(
         jnp.bfloat16
@@ -180,8 +169,11 @@
     head_cols = grad_z.shape[1]
     projected = jnp.concatenate([grad_z, grad_x, grad_bc], axis=1)
     reduced = lax.psum_scatter(
-        row_term(events, projected, norm_scale), "ctx", scatter_dimension=0, tiled=True
-    )
+        row_term(events, projected, norm_scale).astype(jnp.bfloat16),
+        "ctx",
+        scatter_dimension=0,
+        tiled=True,
+    ).astype(jnp.float32)
     grad_w_gate = reduced[:, :head_cols]
     grad_w_value = reduced[:, head_cols : 2 * head_cols]
     grad_w_shared = reduced[:, 2 * head_cols :]

time: 365 us -> 197 us (0.54)
  local copies, waits for them, and re-layouts: 91.5 us -> 21.4 us
  waiting for transfers between devices: 141 us -> 83.5 us
  other arithmetic: 44.5 us -> 9.74 us
    dynamic_slice x30 -> x0, local copies, waits for them, and re-layouts: 48.9 us -> none  [one(): lax.dynamic_index_in_dim(a, source, 0, False)]
    add x15 -> x0, other arithmetic: 35.6 us -> none  [combine(): later_part[1] + later_part[0][:, None, None] * earlier_part[1]]
    unnamed x5, waiting for transfers between devices: 102 us -> 70 us
    all_gather x1, waiting for transfers between devices: 25.4 us -> 2.81 us  [entering(): sums = lax.all_gather(block_sum.astype(jnp.bfloat16), axis)]
    mul x15 -> x0, local copies, waits for them, and re-layouts: 19.2 us -> none  [combine(): later_part[0][:, None, None] * earlier_part[1]]
    unnamed x41 -> x49, local copies, waits for them, and re-layouts: 17.2 us -> 19.3 us
  transfers between devices with their start and end apart: 4 -> 4, of which waited for: 3 -> 3; matrix products, arithmetic and copies ran while one was open for 9% -> 17% of each run, Pallas kernels for 0% -> 0%
where the time goes in v1:
time: 197 us; the launch traced here: 196 us
  waiting for transfers between devices  83.5 us (42%)
  blocking collectives  35.6 us (18%)
  matrix products  31 us (16%)
  local copies, waits for them, and re-layouts  21.4 us (11%)
  between operations  14.8 us (8%)
  other arithmetic  9.74 us (5%)
    unnamed x5, waiting for transfers between devices  70 us
    unnamed x1, blocking collectives  35.6 us
    unnamed x49, local copies, waits for them, and re-layouts  19.3 us
    reduce_scatter x1, waiting for transfers between devices, per_device(): lax.psum_scatter(input_part.astype(jnp.bfloat16), 'head', scatter_dimensi...  10.7 us
    dot_general x1, matrix products, ssd_partials(): jnp.einsum('hkts,kshp->kthp', weighted, values_f, precision=highest)  6.11 us
    dot_general x1, matrix products, row_term(): lax.dot_general(events, projected, (((0,), (0,)), ((), ())), preferred_el...  4.46 us
    dot_general x1, matrix products, ssd_partials(): jnp.einsum('kthp,kshp->hkts', grad_y, values_f, precision=highest)  4.4 us
  transfers between devices with their start and end apart: 4, of which 3 were waited for; matrix products, arithmetic and copies ran while one was open for 17% of the time, Pallas kernels for 0%

profile of v1, /device:TPU:0, one launch (start us, length us, event | category | flops | bytes accessed | tf_op | source)
XLA Modules:
  0.0 196.4 jit_solution(11442944935059460116)
XLA Ops:
  7.2 0.0 copy-start
  7.2 0.0 copy-start.17
  7.2 0.0 copy-start.5
  7.2 0.0 all-gather.3.cloned.1.call-start
  7.2 0.9 reshape.406
  8.1 0.6 reduce-window.6
  8.7 0.2 slice_reduce_fusion
  8.9 0.1 copy.63
  9.0 0.1 broadcast.197
  9.2 0.3 multiply_reduce_fusion.2
  9.5 2.1 %copy.66 = bf16[256,1024]{0,1:T(8,128)(2,1)} copy(bf16[256,1024]{1,0:T(8,128)(2,1)} %param.13) | data formatting | bytes 1048576 | tf_op args[2]
  11.5 2.1 %copy.60 = bf16[256,1024]{0,1:T(8,128)(2,1)} copy(bf16[256,1024]{1,0:T(8,128)(2,1)} %param.14) | data formatting | bytes 1048576 | tf_op args[3]
  13.6 2.5 %divide_multiply_fusion = (f32[256,1024]{0,1:T(8,128)}, f32[256,1024]{0,1:T(8,128)S(1)}) fusion(bf16[256,1024]{0,1:T(8,128)(2,1)} %copy.66, bf16[256,1024]{0,1:T(8,128)(2,1)} %copy.60, f32[256,16]{0,1:T(8,128)S(1)} %bitcast.140), kind=kLoop, calls=%fused_computation.49 | loop fusion | flops 2097152 | bytes 3162112 | tf_op jit(solution)/shard_map/mul | solution.py:62
  16.1 1.3 fusion.48
  17.4 0.0 all-gather.3.cloned.1.call-update
  17.5 0.0 reduce-scatter.6.cloned.1.call-start
  17.6 0.1 exponential_bitcast_fusion
  17.7 0.0 copy-done.17
  17.7 0.6 dynamic-slice.2
  18.9 0.2 dynamic-update-slice
  19.2 35.6 %all-reduce = f32[256]{0:T(256)S(1)} all-reduce(f32[256]{0:T(256)S(1)} %dynamic-update-slice), channel_id=2, replica_groups=mesh['ctx'=16,'head'=2] {'ctx'}, use_global_device_ids=true, to_apply=%add | all-reduce | flops 256 | bytes 2048
  54.7 0.1 reshape.418
  54.8 2.0 %copy.64 = bf16[256,1024]{0,1:T(8,128)(2,1)} copy(bf16[256,1024]{1,0:T(8,128)(2,1)} %param.12) | data formatting | bytes 1048576 | tf_op args[1]
  56.9 0.1 select_reduce_fusion
  57.0 2.1 %convolution_bitcast_fusion.2 = f32[256,128]{0,1:T(8,128)S(1)} fusion(f32[256,16,64]{0,2,1:T(8,128)S(1)} %bitcast.122, f32[1,16,128,64]{2,3,1,0:T(8,128)} %param.18), kind=kOutput, calls=%fused_computation.37 | convolution fusion | flops 402653184 | bytes 1703936 | tf_op jit(solution)/shard_map/kthp,khnp->ktn/dot_general | solution.py:67
  59.1 0.0 copy-done.11
  59.1 0.6 subtract_exponential_fusion
  59.7 0.7 exponential_select_fusion.1
  60.4 0.9 fusion.69
  61.3 4.4 %multiply_reduce_fusion.1 = f32[256,256]{1,0:T(8,128)S(1)} fusion(f32[256,16,64]{0,2,1:T(8,128)} %bitcast.129, bf16[256,16,64]{0,2,1:T(8,128)(2,1)} %bitcast.124, f32[16,256]{1,0:T(8,128)S(1)} %bitcast_add_fusion, pred[256,256]{1,0:T(8,128)(4,1)S(1)} %iota_compare_fusion), kind=kOutput, calls=%fused_computation.3 | convolution fusion | flops 810483712 | bytes 1916928 | tf_op jit(solution)/shard_map/kthp,kshp->hkts/dot_general | solution.py:64
  65.7 1.0 convolution_add_fusion.2
  66.7 1.6 fusion.70
  68.3 2.8 %all-gather.3.cloned.1.call-done = bf16[16,16,128,64]{2,3,1,0:T(8,128)(2,1)} async-done(((bf16[1,16,128,64]{2,3,1,0:T(8,128)(2,1)}), bf16[16,16,128,64]{2,3,1,0:T(8,128)(2,1)}) %all-gather.3.cloned.1.call-update) | async-done | bytes 4194320 | tf_op jit(solution)/shard_map/all_gather | solution.py:18
  71.1 3.1 %multiply_reduce_fusion = f32[16,128,64]{1,2,0:T(8,128)S(1)} fusion(bf16[16,16,128,64]{2,3,1,0:T(8,128)(2,1)} %all-gather.3.cloned.1.call-done, f32[16,16]{1,0:T(8,128)} %exponential_select_fusion.1), kind=kLoop, calls=%fused_computation.1 | loop fusion | flops 6160384 | bytes 4719616 | tf_op jit(solution)/shard_map/reduce_sum | solution.py:23
  74.2 1.8 convolution_bitcast_fusion.3
  76.1 0.3 convolution_add_fusion.3
  76.4 0.7 pad_maximum_fusion
  77.1 0.0 reduce-scatter.6.cloned.1.call-update
  77.1 0.2 reduce-scatter.10.cloned.1.call-start
  77.3 0.0 copy-start.9
  77.4 0.0 copy-start.15
  77.4 6.1 %fusion.43 = bf16[1,256,16,64]{1,3,2,0:T(8,128)(2,1)} fusion(bf16[256,16,64]{0,2,1:T(8,128)(2,1)S(1)} %bitcast.126, f32[256,256]{1,0:T(8,128)} %fusion.69, f32[16,256]{1,0:T(8,128)} %copy-done.14, pred[256,256]{1,0:T(8,128)(4,1)} %copy-done.12, f32[256,16,64]{0,2,1:T(8,128)} %bitcast.131, f32[256,16]{0,1:T(8,128)} %bitcast.141, ...), kind=kOutput, calls=%fused_computation.32 | convolution fusion | flops 813170688 | bytes 3506176 | tf_op jit(solution)/shard_map/hkts,kshp->kthp/dot_general | solution.py:57
  83.5 0.6 fusion.23
  84.2 3.9 %fusion.39 = bf16[1,256,16,64]{1,3,2,0:T(8,128)(2,1)S(1)} fusion(f32[1,256,16,64]{1,3,2,0:T(8,128)S(1)} %fusion.23, f32[256,16,64]{0,2,1:T(8,128)S(1)} %bitcast.130, f32[256,256]{1,0:T(8,128)S(1)} %copy-done.9, f32[16,256]{1,0:T(8,128)S(1)} %copy-done.15, pred[256,256]{1,0:T(8,128)(4,1)S(1)} %copy-done.13), kind=kOutput, calls=%fused_computation.30 | convolution fusion | flops 810024960 | bytes 2965504 | tf_op jit(solution)/shard_map/hkst,kshp->kthp/dot_general | solution.py:69
  88.1 0.0 reduce-scatter.6.cloned.1.call-done
  88.1 0.9 convert_element_type.55
  89.0 4.5 %fusion = bf16[1024,2176]{0,1:T(8,128)(2,1)} fusion(bf16[256,1024]{1,0:T(8,128)(2,1)} %param.11, bf16[256,128]{0,1:T(8,128)(2,1)S(1)} %convert_element_type.55, bf16[256,1024]{0,1:T(8,128)(2,1)S(1)} %bitcast.134, bf16[256,1024]{0,1:T(8,128)(2,1)S(1)} %bitcast.132), kind=kOutput, calls=%fused_computation.2 | convolution fusion | flops 1148649472 | bytes 6094848 | tf_op jit(solution)/shard_map/dot_general | solution.py:130
  93.5 6.5 %copy.70 = bf16[1024,2176]{1,0:T(8,128)(2,1)} copy(bf16[1024,2176]{0,1:T(8,128)(2,1)} %fusion) | data formatting | bytes 8912896
  100.0 0.0 reduce-scatter.10.cloned.1.call-update
  100.0 0.0 copy-start.10
  100.0 0.0 reduce-scatter.8.cloned.1.call-start
  100.1 0.0 copy-start.2
  100.1 0.8 fusion.71
  100.8 0.8 copy-done.2
  101.7 0.8 convolution_add_fusion.1
  102.5 1.1 fusion.42
  103.6 0.0 reduce-scatter.8.cloned.1.call-update
  103.6 69.9 %reduce-scatter.10.cloned.1.call-done = bf16[64,2176]{1,0:T(8,128)(2,1)} async-done(((bf16[1024,2176]{1,0:T(8,128)(2,1)}), bf16[64,2176]{1,0:T(8,128)(2,1)}) %reduce-scatter.10.cloned.1.call-update) | async-done | bytes 278544
  173.5 1.3 copy.71
  174.8 0.7 copy.69
  175.5 0.9 fusion.68
  176.4 1.9 copy.68
  178.3 0.9 copy.67
  179.2 10.7 %reduce-scatter.8.cloned.1.call-done = bf16[256,512]{1,0:T(8,128)(2,1)} async-done(((bf16[256,1024]{1,0:T(8,128)(2,1)}), bf16[256,512]{1,0:T(8,128)(2,1)}) %reduce-scatter.8.cloned.1.call-update) | async-done | bytes 262160 | tf_op jit(solution)/shard_map/reduce_scatter | solution.py:165
  (40 shorter events, 0.2 us)
Async XLA Ops:
  7.2 92.9 %copy-start = (bf16[1024,1024]{1,0:T(8,128)(2,1)S(1)}, bf16[1024,1024]{1,0:T(8,128)(2,1)}, u32[]{:S(2)}) copy-start(bf16[1024,1024]{1,0:T(8,128)(2,1)} %param.19) | copy-start | bytes 6291460
  7.2 10.5 %copy-start.17 = (u32[32]{0:T(128)S(1)}, u32[32]{0:T(128)}, u32[]{:S(2)}) copy-start(u32[32]{0:T(128)} %constant.43) | copy-start | bytes 388
  7.2 8.9 %copy-start.5 = (bf16[256,128]{1,0:T(8,128)(2,1)S(1)}, bf16[256,128]{1,0:T(8,128)(2,1)}, u32[]{:S(2)}) copy-start(bf16[256,128]{1,0:T(8,128)(2,1)} %param.16) | copy-start | bytes 196612
  7.2 63.9 %all-gather.3.cloned.1.call-start = ((), (), s32[]{:S(2)}) async-start(), calls=%async_computation.3 | async-start | bytes 4456448 | tf_op jit(solution)/shard_map/all_gather | solution.py:18
  9.2 50.0 %copy-start.11 = (f32[1,256,16]{1,2,0:T(8,128)}, f32[1,256,16]{1,2,0:T(8,128)S(1)}, u32[]{:S(2)}) copy-start(f32[1,256,16]{1,2,0:T(8,128)S(1)} %copy.81) | copy-start | bytes 49156
  11.5 48.8 %copy-start.6 = (bf16[256,128]{1,0:T(8,128)(2,1)S(1)}, bf16[256,128]{1,0:T(8,128)(2,1)}, u32[]{:S(2)}) copy-start(bf16[256,128]{1,0:T(8,128)(2,1)} %param.15) | copy-start | bytes 196612
  17.5 70.6 %reduce-scatter.6.cloned.1.call-start = ((), (), s32[]{:S(2)}) async-start(), calls=%async_computation.4 | async-start | bytes 393216 | tf_op jit(solution)/shard_map/reduce_scatter | solution.py:159
  56.9 8.8 %copy-start.12 = (pred[256,256]{1,0:T(8,128)(4,1)}, pred[256,256]{1,0:T(8,128)(4,1)S(1)}, u32[]{:S(2)}) copy-start(pred[256,256]{1,0:T(8,128)(4,1)S(1)} %iota_compare_fusion) | copy-start | bytes 196612
  60.4 6.3 %copy-start.14 = (f32[16,256]{1,0:T(8,128)}, f32[16,256]{1,0:T(8,128)S(1)}, u32[]{:S(2)}) copy-start(f32[16,256]{1,0:T(8,128)S(1)} %bitcast_add_fusion) | copy-start | bytes 49156
  61.3 5.4 %copy-start.1 = (f32[1,16,128,64]{2,3,1,0:T(8,128)S(1)}, f32[1,16,128,64]{2,3,1,0:T(8,128)}, u32[]{:S(2)}) copy-start(f32[1,16,128,64]{2,3,1,0:T(8,128)} %param.18) | copy-start | bytes 1572868
  65.7 8.5 %copy-start.3 = (bf16[256,1024]{0,1:T(8,128)(2,1)S(1)}, bf16[256,1024]{0,1:T(8,128)(2,1)}, u32[]{:S(2)}) copy-start(bf16[256,1024]{0,1:T(8,128)(2,1)} %copy.64) | copy-start | bytes 1572868
  71.1 5.2 %copy-start.8 = (f32[256,128]{0,1:T(8,128)S(1)}, f32[256,128]{0,1:T(8,128)}, u32[]{:S(2)}) copy-start(f32[256,128]{0,1:T(8,128)} %convolution_add_fusion.2) | copy-start | bytes 393220
  77.1 96.4 %reduce-scatter.10.cloned.1.call-start = ((), (), s32[]{:S(2)}) async-start(), calls=%async_computation.6 | async-start | bytes 4734976
  77.3 6.2 %copy-start.16 = (f32[16]{0:T(128)S(1)}, f32[16]{0:T(128)}, u32[]{:S(2)}) copy-start(f32[16]{0:T(128)} %subtract_exponential_fusion) | copy-start | bytes 196
  77.3 6.8 %copy-start.4 = (f32[256,1024]{0,1:T(8,128)S(1)}, f32[256,1024]{0,1:T(8,128)}, u32[]{:S(2)}) copy-start(f32[256,1024]{0,1:T(8,128)} %get-tuple-element.58) | copy-start | bytes 3145732
  77.3 6.8 %copy-start.9 = (f32[256,256]{1,0:T(8,128)S(1)}, f32[256,256]{1,0:T(8,128)}, u32[]{:S(2)}) copy-start(f32[256,256]{1,0:T(8,128)} %fusion.69) | copy-start | bytes 786436
  77.4 6.8 %copy-start.13 = (pred[256,256]{1,0:T(8,128)(4,1)S(1)}, pred[256,256]{1,0:T(8,128)(4,1)}, u32[]{:S(2)}) copy-start(pred[256,256]{1,0:T(8,128)(4,1)} %copy-done.12) | copy-start | bytes 196612
  77.4 6.8 %copy-start.15 = (f32[16,256]{1,0:T(8,128)S(1)}, f32[16,256]{1,0:T(8,128)}, u32[]{:S(2)}) copy-start(f32[16,256]{1,0:T(8,128)} %copy-done.14) | copy-start | bytes 49156
  83.5 5.5 %copy-start.7 = (bf16[1,256,16,64]{1,3,2,0:T(8,128)(2,1)S(1)}, bf16[1,256,16,64]{1,3,2,0:T(8,128)(2,1)}, u32[]{:S(2)}) copy-start(bf16[1,256,16,64]{1,3,2,0:T(8,128)(2,1)} %fusion.43) | copy-start | bytes 1572868
  100.0 2.5 %copy-start.10 = (bf16[1024,128]{1,0:T(8,128)(2,1)S(1)}, bf16[1024,128]{1,0:T(8,128)(2,1)}, u32[]{:S(2)}) copy-start(bf16[1024,128]{1,0:T(8,128)(2,1)} %param.21) | copy-start | bytes 786436
  100.0 89.9 %reduce-scatter.8.cloned.1.call-start = ((), (), s32[]{:S(2)}) async-start(), calls=%async_computation.5 | async-start | bytes 786432 | tf_op jit(solution)/shard_map/reduce_scatter | solution.py:165
  100.1 1.6 copy-start.2
Sparse Core Ops, SparseCore 0:
  17.6 53.4 all-gather.2
  77.2 10.1 reduce-scatter.5
  100.1 73.3 reduce-scatter.9
  176.2 13.6 reduce-scatter.7

commit v2 on v1

v2 whole, which is shorter than its diff:
```python
import functools
import math

import jax
import jax.numpy as jnp
from jax import lax
from jax.experimental import pallas as pl
from jax.experimental.pallas import tpu as pltpu
from jax.sharding import PartitionSpec as P

F32 = jnp.float32
BF16 = jnp.bfloat16
HIGHEST = lax.Precision.HIGHEST
MESH = pl.DeviceIdType.MESH
LANES = 128


def dot(a, b, dims=(1, 0), precision=None):
    return lax.dot_general(
        a,
        b,
        (((dims[0],), (dims[1],)), ((), ())),
        preferred_element_type=F32,
        precision=precision,
    )


def split_orders(bits):
    plain = list(range(bits))
    swapped = list(plain)
    if bits >= 3:
        swapped[1], swapped[2] = swapped[2], swapped[1]
    return plain, swapped


def mixer_kernel(cfg, *refs):
    n_ctx, n_head, widths, shared_cols, scale = cfg
    bits = n_ctx.bit_length() - 1
    chunks = len(widths)
    refs = list(refs)
    (ev, x_in, gate, gout, b_in, c_in, ld_in, ent, wg, wv, ws) = refs[:11]
    (o_in, o_g, o_v, o_s) = refs[11:15]
    it = iter(refs[15:])
    cumx, rowc, dyb, sdy, entb, gz, gxp, gxb, psum, acc, evt = [next(it) for _ in range(11)]
    tf, tsend, dsend, inc = [next(it) for _ in range(4)]
    crecv = [next(it) for _ in range(bits)]
    drecv = [next(it) for _ in range(bits)]
    csend = [next(it) for _ in range(bits - 1)]
    dnext = [next(it) for _ in range(bits - 1)]
    ifar = next(it)
    held = [[next(it) for _ in range(bits)] for _ in range(chunks)]
    land = [[next(it) for _ in range(bits)] for _ in range(chunks)]
    bcs, bcr, gis, gir = [next(it) for _ in range(4)]
    c_ss, c_rs, d_ss, d_rs, w_ss, w_rs, b_ss, b_rs, g_ss, g_rs = [next(it) for _ in range(10)]

    length, cols = x_in.shape
    state = b_in.shape[1]
    heads = ld_in.shape[0]
    width = cols // heads
    half = cols // 2
    rows = ev.shape[1] // n_ctx
    out_cols = ev.shape[1] // n_head
    pairs = cols // LANES
    per_pair = LANES // width

    me = lax.axis_index("ctx")
    hid = lax.axis_index("head")
    bit = [lax.rem(me // (1 << b), 2) for b in range(bits)]
    partner = [me + (1 - 2 * bit[b]) * (1 << b) for b in range(bits)]
    peers = [lax.rem(hid + r, n_head) for r in range(1, n_head)]
    core = bit[0]
    started = []

    def send(src, dst, ss, rs, ctx_id, head_id):
        copy = pltpu.make_async_remote_copy(
            src_ref=src,
            dst_ref=dst,
            send_sem=ss,
            recv_sem=rs,
            device_id=(ctx_id, head_id),
            device_id_type=MESH,
        )
        copy.start()
        started.append(copy)
        return copy

    barrier = pltpu.get_barrier_semaphore()
    for p in partner:
        pl.semaphore_signal(barrier, inc=1, device_id=(p, hid), device_id_type=MESH)
    for p in peers:
        pl.semaphore_signal(barrier, inc=1, device_id=(me, p), device_id_type=MESH)

    t_id = lax.broadcasted_iota(jnp.int32, (length, length), 0)
    s_id = lax.broadcasted_iota(jnp.int32, (length, length), 1)
    tril = t_id >= s_id
    triu = t_id <= s_id
    ld = ld_in[...]
    colcum = dot(tril.astype(F32), ld, (1, 1), HIGHEST)
    pick = (
        lax.broadcasted_iota(jnp.int32, (heads, cols), 1) // width
        == lax.broadcasted_iota(jnp.int32, (heads, cols), 0)
    ).astype(F32)
    cumx[...] = dot(colcum, pick, (1, 0), HIGHEST)
    rowc[...] = dot(ld, triu.astype(F32), (1, 0), HIGHEST)
    total = cumx[length - 1 : length, :]

    def at(k):
        return pl.ds(pl.multiple_of(k * LANES, LANES), LANES)

    def before(k, carry):
        sl = at(k)
        g = gate[:, sl].astype(F32)
        dy = gout[:, sl].astype(F32) * g * (1.0 / (1.0 + jnp.exp(-g)))
        dyb[:, sl] = dy.astype(BF16)
        sdy[:, sl] = (dy * jnp.exp(cumx[:, sl])).astype(BF16)
        return carry

    lax.fori_loop(0, pairs, before, 0)
    terms = dot(c_in[...], sdy[...], (0, 0))
    decays = jnp.broadcast_to(jnp.exp(total), (8, cols))
    for h in range(2):
        part = terms[:, h * half : (h + 1) * half]
        tf[h] = part
        tsend[h] = part.astype(BF16)
        dsend[h] = decays[:, h * half : (h + 1) * half]

    pl.semaphore_wait(barrier, bits + n_head - 1)

    flight = {}
    flight[0] = (
        send(tsend.at[1 - core], crecv[0], c_ss.at[0], c_rs.at[0], partner[0], hid),
        send(dsend.at[1 - core], drecv[0], d_ss.at[0], d_rs.at[0], partner[0], hid),
    )
    chain = {}

    def carry_step(k):
        if k == bits:
            flight[bits].wait_recv()
            return
        for copy in flight[k]:
            copy.wait_recv()
        other, other_d = crecv[k][...].astype(F32), drecv[k][0:1, :]
        early = bit[k] == 0
        if k == 0:
            mine, mine_d = tf[core], dsend[core][0:1, :]
            first = jnp.where(early, mine, other)
            last = jnp.where(early, other, mine)
            first_d = jnp.where(early, mine_d, other_d)
            last_d = jnp.where(early, other_d, mine_d)
            chain["last"], chain["last_d"] = last, last_d
            chain["t"] = first + first_d * last
            chain["d"] = first_d * last_d
            chain["x"] = jnp.zeros_like(last)
            chain["q"] = jnp.ones_like(last_d)
        else:
            t, d = chain["t"], chain["d"]
            chain["x"] = jnp.where(early, chain["x"] + chain["q"] * other, chain["x"])
            chain["q"] = jnp.where(early, chain["q"] * other_d, chain["q"])
            chain["t"] = jnp.where(early, t + d * other, other + other_d * t)
            chain["d"] = d * other_d
        if k < bits - 1:
            csend[k][...] = chain["t"].astype(BF16)
            dnext[k][...] = jnp.broadcast_to(chain["d"], (8, half))
            flight[k + 1] = (
                send(csend[k], crecv[k + 1], c_ss.at[k + 1], c_rs.at[k + 1], partner[k + 1], hid),
                send(dnext[k], drecv[k + 1], d_ss.at[k + 1], d_rs.at[k + 1], partner[k + 1], hid),
            )
        else:
            x = chain["x"]
            deeper = chain["last"] + chain["last_d"] * x
            ifar[...] = jnp.where(core == 0, x, deeper).astype(BF16)
            flight[bits] = send(
                ifar, inc.at[core], c_ss.at[bits], c_rs.at[bits], partner[0], hid
            )
            inc[core] = jnp.where(core == 0, deeper, x).astype(BF16)

    orders = split_orders(bits)
    rs_flight = {}

    def rs_send(c, k):
        order = orders[c % 2]
        b = order[k]
        count = n_ctx >> (k + 1)
        rs_flight[c, k] = send(
            held[c][k].at[pl.ds((1 - bit[b]) * count, count)],
            land[c][k],
            w_ss.at[c * bits + k],
            w_rs.at[c * bits + k],
            partner[b],
            hid,
        )

    def rs_begin(c, values):
        order = orders[c % 2]
        tile = min(256, ev.shape[1])
        for start in range(0, ev.shape[1], tile):
            part = dot(evt[start : start + tile, :], values).astype(BF16)
            for j in range(tile // rows):
                index = start // rows + j
                place = 0
                for k, b in enumerate(order):
                    place += ((index >> b) & 1) << (bits - 1 - k)
                held[c][0][place] = part[j * rows : (j + 1) * rows, :]
        rs_send(c, 0)

    outs = []

    def rs_step(c, k):
        order = orders[c % 2]
        b = order[k]
        count = n_ctx >> (k + 1)
        rs_flight[c, k].wait_recv()
        kept = held[c][k][pl.ds(bit[b] * count, count)].astype(F32) + land[c][k][...].astype(F32)
        if k < bits - 1:
            held[c][k + 1][...] = kept.astype(BF16)
            rs_send(c, k + 1)
        else:
            out, low, high = outs[c]
            out[:, low:high] = kept[0] * scale

    per_kind = (chunks - 1) // 2
    step = cols // per_kind
    for out in (o_g, o_v):
        for j in range(per_kind):
            outs.append((out, j * step, (j + 1) * step))
    outs.append((o_s, 0, widths[-1]))

    scores = dot(c_in[...], b_in[...], (1, 1))
    scores_t = dot(b_in[...], c_in[...], (1, 1))
    entb[...] = ent[...].astype(BF16)
    psum[...] = jnp.zeros_like(psum)
    lane = lax.broadcasted_iota(jnp.int32, (length, LANES), 1) // width

    def pair(k, carry):
        sl = at(k)
        x = x_in[:, sl]
        cum = cumx[:, sl]
        dyv = dyb[:, sl]
        dyf = dyv.astype(F32)
        y = jnp.exp(cum) * dot(c_in[...], entb[sl, :], (1, 1))
        gx = jnp.zeros((length, LANES), F32)
        both = psum[...]
        for q in range(per_pair):
            col = cum[:, q * width : q * width + 1]
            row = rowc[pl.ds(k * per_pair + q, 1), :]
            gap = col - row
            decay = jnp.where(tril, jnp.exp(jnp.minimum(gap, 0.0)), 0.0)
            decay_t = jnp.where(triu, jnp.exp(jnp.minimum(-gap, 0.0)), 0.0)
            own = lane == q
            y = y + jnp.where(own, dot((decay * scores).astype(BF16), x), 0.0)
            gx = gx + jnp.where(own, dot((decay_t * scores_t).astype(BF16), dyv), 0.0)
            both = both + decay * dot(jnp.where(own, dyf, 0.0).astype(BF16), x, (1, 1))
        psum[...] = both
        gxp[:, sl] = gx
        g = gate[:, sl].astype(F32)
        sig = 1.0 / (1.0 + jnp.exp(-g))
        gz[:, sl] = (gout[:, sl].astype(F32) * y * sig * (1.0 + g * (1.0 - sig))).astype(BF16)
        return carry

    cuts = [0, pairs // 4, pairs // 2, pairs]

    def some_pairs(i):
        if cuts[i + 1] > cuts[i]:
            lax.fori_loop(cuts[i], cuts[i + 1], pair, 0)

    evt[...] = ev[...].T
    some_pairs(0)
    carry_step(0)
    some_pairs(1)
    carry_step(1)
    some_pairs(2)
    carry_step(2)
    for c in range(per_kind):
        rs_begin(c, gz[:, c * step : (c + 1) * step])
    for k in range(3, bits):
        carry_step(k)
    acc[...] = dot(gz[...], wg[...], (1, 1))
    grad_c = dot(psum[...].astype(BF16), b_in[...]) + dot(sdy[...], entb[...])
    grad_b = dot(psum[...].T.astype(BF16), c_in[...])
    for c in range(per_kind):
        rs_step(c, 0)
    carry_step(bits)

    for h in range(2):
        cut = slice(h * half, (h + 1) * half)
        to_end = jnp.exp(total[:, cut] - cumx[:, cut])
        gxb[:, cut] = (gxp[:, cut] + to_end * dot(b_in[...], inc[h])).astype(BF16)
        scaled = (x_in[:, cut].astype(F32) * to_end).astype(BF16)
        grad_b = grad_b + dot(scaled, inc[h], (1, 1))
    bcs[:, 0:state] = grad_b.astype(BF16)
    bcs[:, state : 2 * state] = grad_c.astype(BF16)
    bc_copies = [
        send(bcs, bcr.at[r], b_ss.at[r], b_rs.at[r], me, p) for r, p in enumerate(peers)
    ]
    for c in range(per_kind):
        rs_begin(per_kind + c, gxb[:, c * step : (c + 1) * step])
    for c in range(per_kind):
        rs_step(c, 1)
    acc[...] += dot(gxb[...], wv[...], (1, 1))
    grad_bc = jnp.concatenate([grad_b, grad_c], axis=1)
    for r, copy in enumerate(bc_copies):
        copy.wait_recv()
        grad_bc = grad_bc + bcr[r].astype(F32)
    sel = (
        lax.broadcasted_iota(jnp.int32, (2 * state, widths[-1]), 0)
        == lax.broadcasted_iota(jnp.int32, (2 * state, widths[-1]), 1) + hid * shared_cols
    ) & (lax.broadcasted_iota(jnp.int32, (2 * state, widths[-1]), 1) < shared_cols)
    shared = dot(grad_bc.astype(BF16), sel.astype(F32).astype(BF16)).astype(BF16)
    rs_begin(chunks - 1, shared)
    full = acc[...] + dot(shared, ws[...], (1, 1))
    for j in range(n_head):
        gis[j] = full[:, j * out_cols : (j + 1) * out_cols].astype(BF16)
    gi_copies = [
        send(gis.at[p], gir.at[r], g_ss.at[r], g_rs.at[r], me, p) for r, p in enumerate(peers)
    ]
    value_chunks = range(per_kind, chunks)
    for k in range(bits):
        for c in value_chunks:
            rs_step(c, k)
        if k + 2 < bits:
            for c in range(per_kind):
                rs_step(c, k + 2)
    grad_in = gis[hid].astype(F32)
    for r, copy in enumerate(gi_copies):
        copy.wait_recv()
        grad_in = grad_in + gir[r].astype(F32)
    o_in[...] = grad_in.astype(BF16)
    for copy in started:
        copy.wait_send()


def per_device(
    n_ctx,
    n_head,
    events,
    ssm_input,
    gate_input,
    grad_out,
    shared_b,
    shared_c,
    log_decay,
    entry_state,
    w_gate,
    w_value,
    w_shared,
):
    length, cols = ssm_input.shape
    depth = events.shape[1]
    state = shared_b.shape[1]
    shared_cols = w_shared.shape[1]
    shared_wide = -(-shared_cols // LANES) * LANES
    if shared_wide > shared_cols:
        w_shared = jnp.pad(w_shared, ((0, 0), (0, shared_wide - shared_cols)))
    bits = n_ctx.bit_length() - 1
    rows = depth // n_ctx
    per_kind = 2
    widths = [cols // per_kind] * (2 * per_kind) + [shared_wide]
    half = cols // 2
    entry = entry_state[0].transpose(0, 2, 1).reshape(cols, state)
    scale = 1.0 / math.sqrt(length * n_ctx)
    v = pltpu.VMEM
    dma = pltpu.SemaphoreType.DMA
    peers = n_head - 1
    scratch = [
        v((length, cols), F32),
        v((log_decay.shape[0], length), F32),
        v((length, cols), BF16),
        v((length, cols), BF16),
        v((cols, state), BF16),
        v((length, cols), BF16),
        v((length, cols), F32),
        v((length, cols), BF16),
        v((length, length), F32),
        v((length, depth), F32),
        v((depth, length), BF16),
        v((2, state, half), F32),
        v((2, state, half), BF16),
        v((2, 8, half), F32),
        v((2, state, half), BF16),
    ]
    scratch += [v((state, half), BF16) for _ in range(bits)]
    scratch += [v((8, half), F32) for _ in range(bits)]
    scratch += [v((state, half), BF16) for _ in range(bits - 1)]
    scratch += [v((8, half), F32) for _ in range(bits - 1)]
    scratch += [v((state, half), BF16)]
    for w in widths:
        scratch += [v((n_ctx >> k, rows, w), BF16) for k in range(bits)]
    for w in widths:
        scratch += [v((n_ctx >> (k + 1), rows, w), BF16) for k in range(bits)]
    scratch += [
        v((length, 2 * state), BF16),
        v((peers, length, 2 * state), BF16),
        v((n_head, length, depth // n_head), BF16),
        v((peers, length, depth // n_head), BF16),
        dma((bits + 1,)),
        dma((bits + 1,)),
        dma((bits,)),
        dma((bits,)),
        dma((len(widths) * bits,)),
        dma((len(widths) * bits,)),
        dma((peers,)),
        dma((peers,)),
        dma((peers,)),
        dma((peers,)),
    ]
    whole = pl.BlockSpec(memory_space=pltpu.VMEM)
    flops = 2 * length * (5 * state * cols + 3 * length * cols + 4 * depth * cols)
    grad_input, grad_w_gate, grad_w_value, grad_w_shared = pl.pallas_call(
        functools.partial(mixer_kernel, (n_ctx, n_head, widths, shared_cols, scale)),
        out_shape=(
            jax.ShapeDtypeStruct((length, depth // n_head), BF16),
            jax.ShapeDtypeStruct((rows, cols), F32),
            jax.ShapeDtypeStruct((rows, cols), F32),
            jax.ShapeDtypeStruct((rows, shared_wide), F32),
        ),
        in_specs=[whole] * 11,
        out_specs=(whole,) * 4,
        scratch_shapes=scratch,
        compiler_params=pltpu.CompilerParams(
            collective_id=0, has_side_effects=True, vmem_limit_bytes=58 * 1024 * 1024
        ),
        cost_estimate=pl.CostEstimate(
            flops=flops, bytes_accessed=8 * 1024 * 1024, transcendentals=length * length * 32
        ),
        name="mixer",
    )(
        events,
        ssm_input,
        gate_input,
        grad_out,
        shared_b,
        shared_c,
        log_decay,
        entry,
        w_gate,
        w_value,
        w_shared,
    )
    return (grad_input, grad_w_gate, grad_w_value, grad_w_shared[:, :shared_cols])


def solution(mesh):
    placed = (
        P("ctx", None),
        P("ctx", "head"),
        P("ctx", "head"),
        P("ctx", "head"),
        P("ctx", None),
        P("ctx", None),
        P("head", "ctx"),
        P("ctx", "head", None, None),
        P(None, "head"),
        P(None, "head"),
        P(None, "head"),
    )
    return jax.shard_map(
        functools.partial(per_device, mesh.shape["ctx"], mesh.shape["head"]),
        mesh=mesh,
        in_specs=placed,
        out_specs=(P("ctx", "head"), P("ctx", "head"), P("ctx", "head"), P("ctx", "head")),
        check_vma=False,
    )
```

time: 197 us -> 65.3 us (0.33)
  waiting for transfers between devices: 83.5 us -> 0 us
  Pallas kernels: 0 us -> 58 us
  blocking collectives: 35.6 us -> 0 us
  matrix products: 31 us -> 0 us
  local copies, waits for them, and re-layouts: 21.4 us -> 6.38 us
  between operations: 14.8 us -> 0.64 us
  other arithmetic: 9.74 us -> 0 us
    unnamed x5 -> x0, waiting for transfers between devices: 70 us -> none
    pallas_call x0 -> x1, Pallas kernels: none -> 58 us  [per_device(): pl.pallas_call(functools.partial(mixer_kernel, (n_ctx, n_head, widths, sh...]
    unnamed x1 -> x0, blocking collectives: 35.6 us -> none
    dot_general x14 -> x0, matrix products: 29.4 us -> none  [the longest x1 6.11 us: ssd_partials(): jnp.einsum('hkts,kshp->kthp', weighted, values_f, precision=highest)]
    unnamed x49 -> x4, local copies, waits for them, and re-layouts: 19.3 us -> 6.38 us
    reduce_scatter x2 -> x0, waiting for transfers between devices: 10.7 us -> none  [the longest x1 10.7 us: per_device(): lax.psum_scatter(input_part.astype(jnp.bfloat16), 'head', scatter_dimensi...]
    reduce_sum x2 -> x0, other arithmetic: 3.24 us -> none  [the longest x1 3.13 us: entering(): return jnp.sum(weight[:, :, None, None] * sums.astype(jnp.float32), axis=0)]
    all_gather x1 -> x0, waiting for transfers between devices: 2.81 us -> none  [entering(): sums = lax.all_gather(block_sum.astype(jnp.bfloat16), axis)]
  transfers between devices with their start and end apart: 4 -> 0, of which waited for: 3 -> 0; matrix products, arithmetic and copies ran while one was open for 17% -> 0% of each run, Pallas kernels for 0% -> 0%
where the time goes in v2:
time: 65.3 us; the launch traced here: 65 us
  Pallas kernels  58 us (89%)
  local copies, waits for them, and re-layouts  6.38 us (10%)
    pallas_call x1, Pallas kernels, per_device(): pl.pallas_call(functools.partial(mixer_kernel, (n_ctx, n_head, widths, sh...  58 us
    unnamed x4, local copies, waits for them, and re-layouts  6.38 us

profile of v2, /device:TPU:0, one launch (start us, length us, event | category | flops | bytes accessed | tf_op | source)
XLA Modules:
  0.0 65.0 jit_solution(5943459157182185473)
XLA Ops:
  0.6 58.0 %mixer.1 = (bf16[256,512]{1,0:T(8,128)(2,1)}, f32[64,1024]{1,0:T(8,128)}, f32[64,1024]{1,0:T(8,128)}, f32[64,128]{1,0:T(8,128)}) custom-call(bf16[256,1024]{1,0:T(8,128)(2,1)} %refs_0_.1, bf16[256,1024]{1,0:T(8,128)(2,1)} %refs_1_.1, bf16[256,1024]{1,0:T(8,128)(2,1)} %refs_2_.1, bf16[256,1024]{1,0:T(8,128)(2,1)} %refs_3_.1, bf16[256,128]{1,0:T(8,128)(2,1)} %refs_4_.1, ...), custom_call_target="tpu_custom_call" | custom-call | flops 2885681152 | bytes 8388608 | tf_op jit(solution)/shard_map/mixer/pallas_call | solution.py:408
  58.6 1.7 %copy.19 = bf16[256,512]{1,0:T(8,128)(2,1)} copy(bf16[256,512]{1,0:T(8,128)(2,1)} %get-tuple-element.8) | data formatting | bytes 524288
  60.3 1.7 %copy.20 = f32[64,1024]{1,0:T(8,128)} copy(f32[64,1024]{1,0:T(8,128)} %get-tuple-element.9) | data formatting | bytes 524288
  62.0 1.7 %copy.21 = f32[64,1024]{1,0:T(8,128)} copy(f32[64,1024]{1,0:T(8,128)} %get-tuple-element.10) | data formatting | bytes 524288
  63.6 1.4 %copy.22 = f32[64,128]{1,0:T(8,128)} copy(f32[64,128]{1,0:T(8,128)} %get-tuple-element.11) | data formatting | bytes 65536

commit v3 on v2

--- a/solution.py
+++ b/solution.py
@@ -34,13 +34,14 @@
 
 
 def mixer_kernel(cfg, *refs):
-    n_ctx, n_head, widths, shared_cols, scale = cfg
+    n_ctx, n_head, widths, shared_cols = cfg
     bits = n_ctx.bit_length() - 1
     chunks = len(widths)
     refs = list(refs)
-    (ev, x_in, gate, gout, b_in, c_in, ld_in, ent, wg, wv, ws) = refs[:11]
+    (ev_h, x_in, gate, gout, b_in, c_in, ld_in, ent_h, wg_h, wv_h, ws_h) = refs[:11]
     (o_in, o_g, o_v, o_s) = refs[11:15]
-    it = iter(refs[15:])
+    ev, ent, wg, wv, ws, in_sems = refs[15:21]
+    it = iter(refs[21:])
     cumx, rowc, dyb, sdy, entb, gz, gxp, gxb, psum, acc, evt = [next(it) for _ in range(11)]
     tf, tsend, dsend, inc = [next(it) for _ in range(4)]
     crecv = [next(it) for _ in range(bits)]
@@ -70,6 +71,12 @@
     peers = [lax.rem(hid + r, n_head) for r in range(1, n_head)]
     core = bit[0]
     started = []
+    fetch = [
+        pltpu.make_async_copy(src, dst, in_sems.at[i])
+        for i, (src, dst) in enumerate(
+            ((ent_h, ent), (ev_h, ev), (wg_h, wg), (wv_h, wv), (ws_h, ws))
+        )
+    ]
 
     def send(src, dst, ss, rs, ctx_id, head_id):
         copy = pltpu.make_async_remote_copy(
@@ -89,6 +96,9 @@
         pl.semaphore_signal(barrier, inc=1, device_id=(p, hid), device_id_type=MESH)
     for p in peers:
         pl.semaphore_signal(barrier, inc=1, device_id=(me, p), device_id_type=MESH)
+
+    for copy in fetch:
+        copy.start()
 
     t_id = lax.broadcasted_iota(jnp.int32, (length, length), 0)
     s_id = lax.broadcasted_iota(jnp.int32, (length, length), 1)
@@ -216,7 +226,7 @@
             rs_send(c, k + 1)
         else:
             out, low, high = outs[c]
-            out[:, low:high] = kept[0] * scale
+            out[:, low:high] = kept[0]
 
     per_kind = (chunks - 1) // 2
     step = cols // per_kind
@@ -227,6 +237,7 @@
 
     scores = dot(c_in[...], b_in[...], (1, 1))
     scores_t = dot(b_in[...], c_in[...], (1, 1))
+    fetch[0].wait()
     entb[...] = ent[...].astype(BF16)
     psum[...] = jnp.zeros_like(psum)
     lane = lax.broadcasted_iota(jnp.int32, (length, LANES), 1) // width
@@ -257,46 +268,80 @@
         gz[:, sl] = (gout[:, sl].astype(F32) * y * sig * (1.0 + g * (1.0 - sig))).astype(BF16)
         return carry
 
-    cuts = [0, pairs // 4, pairs // 2, pairs]
+    group = pairs // per_kind
+    gates = list(range(per_kind))
+    values = list(range(per_kind, 2 * per_kind))
+    last = chunks - 1
+    reached = [0] * chunks
+
+    def advance(which):
+        for c in which:
+            if reached[c] < bits:
+                rs_step(c, reached[c])
+                reached[c] += 1
 
     def some_pairs(i):
-        if cuts[i + 1] > cuts[i]:
-            lax.fori_loop(cuts[i], cuts[i + 1], pair, 0)
-
-    evt[...] = ev[...].T
+        lax.fori_loop(i * group, (i + 1) * group, pair, 0)
+
+    def gate_begin(c):
+        rs_begin(c, gz[:, c * step : (c + 1) * step])
+
     some_pairs(0)
     carry_step(0)
+    fetch[1].wait()
+    evt[...] = ev[...].T
     some_pairs(1)
     carry_step(1)
-    some_pairs(2)
+    gate_begin(0)
+    for i in range(2, per_kind):
+        some_pairs(i)
+        gate_begin(i - 1)
+        if i == 2:
+            advance(gates[:1])
     carry_step(2)
-    for c in range(per_kind):
-        rs_begin(c, gz[:, c * step : (c + 1) * step])
-    for k in range(3, bits):
-        carry_step(k)
+    gate_begin(per_kind - 1)
+    fetch[2].wait()
     acc[...] = dot(gz[...], wg[...], (1, 1))
     grad_c = dot(psum[...].astype(BF16), b_in[...]) + dot(sdy[...], entb[...])
     grad_b = dot(psum[...].T.astype(BF16), c_in[...])
-    for c in range(per_kind):
-        rs_step(c, 0)
+    advance([c for c in gates[0::2] if reached[c] == 0])
+    for k in range(3, bits):
+        carry_step(k)
+    advance(gates[1::2])
     carry_step(bits)
 
-    for h in range(2):
-        cut = slice(h * half, (h + 1) * half)
+    def later_terms(c):
+        cut = slice(c * step, (c + 1) * step)
+        low = c * step % half
+        into = inc[c * step // half][:, low : low + step]
         to_end = jnp.exp(total[:, cut] - cumx[:, cut])
-        gxb[:, cut] = (gxp[:, cut] + to_end * dot(b_in[...], inc[h])).astype(BF16)
+        gxb[:, cut] = (gxp[:, cut] + to_end * dot(b_in[...], into)).astype(BF16)
         scaled = (x_in[:, cut].astype(F32) * to_end).astype(BF16)
-        grad_b = grad_b + dot(scaled, inc[h], (1, 1))
+        return dot(scaled, into, (1, 1))
+
+    def value_begin(c):
+        rs_begin(per_kind + c, gxb[:, c * step : (c + 1) * step])
+
+    grad_b = grad_b + later_terms(0)
+    value_begin(0)
+    for c in range(1, per_kind):
+        grad_b = grad_b + later_terms(c)
     bcs[:, 0:state] = grad_b.astype(BF16)
     bcs[:, state : 2 * state] = grad_c.astype(BF16)
     bc_copies = [
         send(bcs, bcr.at[r], b_ss.at[r], b_rs.at[r], me, p) for r, p in enumerate(peers)
     ]
-    for c in range(per_kind):
-        rs_begin(per_kind + c, gxb[:, c * step : (c + 1) * step])
-    for c in range(per_kind):
-        rs_step(c, 1)
+    if per_kind > 1:
+        value_begin(1)
+    advance(gates[0::2])
+    advance(values[0:2])
+    for c in range(2, per_kind):
+        value_begin(c)
+    advance(gates[1::2])
+    advance(values[2:])
+    fetch[3].wait()
     acc[...] += dot(gxb[...], wv[...], (1, 1))
+    advance(gates[0::2])
     grad_bc = jnp.concatenate([grad_b, grad_c], axis=1)
     for r, copy in enumerate(bc_copies):
         copy.wait_recv()
@@ -306,20 +351,19 @@
         == lax.broadcasted_iota(jnp.int32, (2 * state, widths[-1]), 1) + hid * shared_cols
     ) & (lax.broadcasted_iota(jnp.int32, (2 * state, widths[-1]), 1) < shared_cols)
     shared = dot(grad_bc.astype(BF16), sel.astype(F32).astype(BF16)).astype(BF16)
-    rs_begin(chunks - 1, shared)
+    rs_begin(last, shared)
+    fetch[4].wait()
     full = acc[...] + dot(shared, ws[...], (1, 1))
     for j in range(n_head):
         gis[j] = full[:, j * out_cols : (j + 1) * out_cols].astype(BF16)
     gi_copies = [
         send(gis.at[p], gir.at[r], g_ss.at[r], g_rs.at[r], me, p) for r, p in enumerate(peers)
     ]
-    value_chunks = range(per_kind, chunks)
-    for k in range(bits):
-        for c in value_chunks:
-            rs_step(c, k)
-        if k + 2 < bits:
-            for c in range(per_kind):
-                rs_step(c, k + 2)
+    advance([last])
+    while min(reached) < bits:
+        advance(values)
+        advance(gates)
+        advance([last])
     grad_in = gis[hid].astype(F32)
     for r, copy in enumerate(gi_copies):
         copy.wait_recv()
@@ -327,6 +371,13 @@
     o_in[...] = grad_in.astype(BF16)
     for copy in started:
         copy.wait_send()
+
+
+def finish_kernel(scale, a, b, c, d, o_a, o_b, o_c, o_d):
+    o_a[...] = a[...]
+    o_b[...] = b[...] * scale
+    o_c[...] = c[...] * scale
+    o_d[...] = d[:, 0 : o_d.shape[1]] * scale
 
 
 def per_device(
@@ -353,7 +404,7 @@
         w_shared = jnp.pad(w_shared, ((0, 0), (0, shared_wide - shared_cols)))
     bits = n_ctx.bit_length() - 1
     rows = depth // n_ctx
-    per_kind = 2
+    per_kind = max(1, min(4, cols // LANES))
     widths = [cols // per_kind] * (2 * per_kind) + [shared_wide]
     half = cols // 2
     entry = entry_state[0].transpose(0, 2, 1).reshape(cols, state)
@@ -362,6 +413,12 @@
     dma = pltpu.SemaphoreType.DMA
     peers = n_head - 1
     scratch = [
+        v(events.shape, BF16),
+        v(entry.shape, F32),
+        v(w_gate.shape, BF16),
+        v(w_value.shape, BF16),
+        v(w_shared.shape, BF16),
+        dma((5,)),
         v((length, cols), F32),
         v((log_decay.shape[0], length), F32),
         v((length, cols), BF16),
@@ -404,16 +461,17 @@
         dma((peers,)),
     ]
     whole = pl.BlockSpec(memory_space=pltpu.VMEM)
+    far = pl.BlockSpec(memory_space=pl.ANY)
     flops = 2 * length * (5 * state * cols + 3 * length * cols + 4 * depth * cols)
-    grad_input, grad_w_gate, grad_w_value, grad_w_shared = pl.pallas_call(
-        functools.partial(mixer_kernel, (n_ctx, n_head, widths, shared_cols, scale)),
+    results = pl.pallas_call(
+        functools.partial(mixer_kernel, (n_ctx, n_head, widths, shared_cols)),
         out_shape=(
             jax.ShapeDtypeStruct((length, depth // n_head), BF16),
             jax.ShapeDtypeStruct((rows, cols), F32),
             jax.ShapeDtypeStruct((rows, cols), F32),
             jax.ShapeDtypeStruct((rows, shared_wide), F32),
         ),
-        in_specs=[whole] * 11,
+        in_specs=[far, *[whole] * 6, far, far, far, far],
         out_specs=(whole,) * 4,
         scratch_shapes=scratch,
         compiler_params=pltpu.CompilerParams(
@@ -436,7 +494,16 @@
         w_value,
         w_shared,
     )
-    return (grad_input, grad_w_gate, grad_w_value, grad_w_shared[:, :shared_cols])
+    return pl.pallas_call(
+        functools.partial(finish_kernel, scale),
+        out_shape=(
+            *[jax.ShapeDtypeStruct(r.shape, r.dtype) for r in results[:3]],
+            jax.ShapeDtypeStruct((rows, shared_cols), F32),
+        ),
+        in_specs=[whole] * 4,
+        out_specs=(whole,) * 4,
+        name="finish",
+    )(*results)
 
 
 def solution(mesh):

time: 65.3 us -> 58.8 us (0.900)
  local copies, waits for them, and re-layouts: 6.38 us -> 0 us
    unnamed x4 -> x0, local copies, waits for them, and re-layouts: 6.38 us -> none
    pallas_call x0 -> x1, Pallas kernels: none -> 2.01 us  [per_device(): pl.pallas_call(functools.partial(finish_kernel, scale), out_shape=(*[jax....]
    pallas_call x1, Pallas kernels: 58 us -> 56 us  [per_device(): pl.pallas_call(functools.partial(mixer_kernel, (n_ctx, n_head, widths, sh...]
where the time goes in v3:
time: 58.8 us; the launch traced here: 58.6 us
  Pallas kernels  58 us (99%)
  between operations  0.64 us (1%)
    pallas_call x1, Pallas kernels, per_device(): pl.pallas_call(functools.partial(mixer_kernel, (n_ctx, n_head, widths, sh...  56 us
    pallas_call x1, Pallas kernels, per_device(): pl.pallas_call(functools.partial(finish_kernel, scale), out_shape=(*[jax....  2.01 us

profile of v3, /device:TPU:0, one launch (start us, length us, event | category | flops | bytes accessed | tf_op | source)
XLA Modules:
  0.0 58.6 jit_solution(16004441087625964104)
XLA Ops:
  0.6 56.0 %mixer.1 = (bf16[256,512]{1,0:T(8,128)(2,1)}, f32[64,1024]{1,0:T(8,128)}, f32[64,1024]{1,0:T(8,128)}, f32[64,128]{1,0:T(8,128)}) custom-call(bf16[256,1024]{1,0:T(8,128)(2,1)} %refs_0_.1, bf16[256,1024]{1,0:T(8,128)(2,1)} %refs_1_.1, bf16[256,1024]{1,0:T(8,128)(2,1)} %refs_2_.1, bf16[256,1024]{1,0:T(8,128)(2,1)} %refs_3_.1, bf16[256,128]{1,0:T(8,128)(2,1)} %refs_4_.1, ...), custom_call_target="tpu_custom_call" | custom-call | flops 2885681152 | bytes 8388608 | tf_op jit(solution)/shard_map/mixer/pallas_call | solution.py:466
  56.6 2.0 %finish.1 = (bf16[256,512]{1,0:T(8,128)(2,1)}, f32[64,1024]{1,0:T(8,128)}, f32[64,1024]{1,0:T(8,128)}, f32[64,128]{1,0:T(8,128)}) custom-call(bf16[256,512]{1,0:T(8,128)(2,1)} %get-tuple-element.8.a, f32[64,1024]{1,0:T(8,128)} %get-tuple-element.9.b, f32[64,1024]{1,0:T(8,128)} %get-tuple-element.10.c, f32[64,128]{1,0:T(8,128)} %get-tuple-element.11.d), custom_call_target="tpu_custom_call" | custom-call | tf_op jit(solution)/shard_map/finish/pallas_call | solution.py:497

commit v4 on v3

--- a/solution.py
+++ b/solution.py
@@ -295,16 +295,15 @@
     gate_begin(0)
     for i in range(2, per_kind):
         some_pairs(i)
+        if i == 2:
+            carry_step(2)
         gate_begin(i - 1)
-        if i == 2:
-            advance(gates[:1])
-    carry_step(2)
+    if per_kind <= 2:
+        carry_step(2)
     gate_begin(per_kind - 1)
-    fetch[2].wait()
-    acc[...] = dot(gz[...], wg[...], (1, 1))
     grad_c = dot(psum[...].astype(BF16), b_in[...]) + dot(sdy[...], entb[...])
     grad_b = dot(psum[...].T.astype(BF16), c_in[...])
-    advance([c for c in gates[0::2] if reached[c] == 0])
+    advance(gates[0::2])
     for k in range(3, bits):
         carry_step(k)
     advance(gates[1::2])
@@ -337,10 +336,11 @@
     advance(values[0:2])
     for c in range(2, per_kind):
         value_begin(c)
+    advance(values[2:])
     advance(gates[1::2])
-    advance(values[2:])
+    fetch[2].wait()
     fetch[3].wait()
-    acc[...] += dot(gxb[...], wv[...], (1, 1))
+    acc[...] = dot(gz[...], wg[...], (1, 1)) + dot(gxb[...], wv[...], (1, 1))
     advance(gates[0::2])
     grad_bc = jnp.concatenate([grad_b, grad_c], axis=1)
     for r, copy in enumerate(bc_copies):

time: 58.8 us -> 58.7 us (level)
  no operation moved by 1% of the time
where the time goes in v4:
time: 58.7 us; the launch traced here: 58.5 us
  Pallas kernels  57.9 us (99%)
  between operations  0.64 us (1%)
    pallas_call x1, Pallas kernels, per_device(): pl.pallas_call(functools.partial(mixer_kernel, (n_ctx, n_head, widths, sh...  55.9 us
    pallas_call x1, Pallas kernels, per_device(): pl.pallas_call(functools.partial(finish_kernel, scale), out_shape=(*[jax....  2.01 us

profile of v4, /device:TPU:0, one launch (start us, length us, event | category | flops | bytes accessed | tf_op | source)
XLA Modules:
  0.0 58.5 jit_solution(5039513151250545246)
XLA Ops:
  0.6 55.9 %mixer.1 = (bf16[256,512]{1,0:T(8,128)(2,1)}, f32[64,1024]{1,0:T(8,128)}, f32[64,1024]{1,0:T(8,128)}, f32[64,128]{1,0:T(8,128)}) custom-call(bf16[256,1024]{1,0:T(8,128)(2,1)} %refs_0_.1, bf16[256,1024]{1,0:T(8,128)(2,1)} %refs_1_.1, bf16[256,1024]{1,0:T(8,128)(2,1)} %refs_2_.1, bf16[256,1024]{1,0:T(8,128)(2,1)} %refs_3_.1, bf16[256,128]{1,0:T(8,128)(2,1)} %refs_4_.1, ...), custom_call_target="tpu_custom_call" | custom-call | flops 2885681152 | bytes 8388608 | tf_op jit(solution)/shard_map/mixer/pallas_call | solution.py:466
  56.5 2.0 %finish.1 = (bf16[256,512]{1,0:T(8,128)(2,1)}, f32[64,1024]{1,0:T(8,128)}, f32[64,1024]{1,0:T(8,128)}, f32[64,128]{1,0:T(8,128)}) custom-call(bf16[256,512]{1,0:T(8,128)(2,1)} %get-tuple-element.8.a, f32[64,1024]{1,0:T(8,128)} %get-tuple-element.9.b, f32[64,1024]{1,0:T(8,128)} %get-tuple-element.10.c, f32[64,128]{1,0:T(8,128)} %get-tuple-element.11.d), custom_call_target="tpu_custom_call" | custom-call | tf_op jit(solution)/shard_map/finish/pallas_call | solution.py:497
